TPU v7x, 32 devices: a whole 2x2x4 slice. The times are simulated.
32 devices in a mesh: tile: 4 (over y, core), rep: 8 (over z, x).
Axes of the slice: x: 2, y: 2, z: 4, core: 2. Of those that a mesh axis runs over, the one named last changes fastest.
Arguments:
- inputs: bfloat16 [8, 8, 32, 32, 256], P('rep', 'tile'), may hold values from -6 to 6
- grad_out: bfloat16 [8, 8, 32, 32, 256], P('rep', 'tile'), may hold values from -6 to 6
- seam_links: int32 [8, 4, 3], P('tile'), may hold values from 0 to 7, as said below
- corner_links: int32 [8, 4, 2], P('tile'), may hold values from 0 to 7, as said below
- dw_weight: float32 [256, 9], replicated, may hold values from -1 to 1
- norm_gain: float32 [256], replicated, may hold values from 0.1 to 1.9
- w_in: bfloat16 [256, 1024], replicated, may hold values from -0.375 to 0.375
- bias_in: float32 [1024], replicated, may hold values from -1 to 1
- w_out: bfloat16 [1024, 256], replicated, may hold values from -0.1875 to 0.1875
- layer_scale: float32 [256], replicated, may hold values from 0.25 to 2
Outputs:
- block_out: bfloat16 [8, 8, 32, 32, 256], P('rep', 'tile')
- x_grad: float32 [8, 8, 32, 32, 256], P('rep', 'tile')
- grad_dw: float32 [256, 9], replicated
- grad_gain: float32 [256], replicated
- grad_w_in: float32 [256, 1024], replicated
- grad_bias: float32 [1024], replicated
- grad_w_out: float32 [1024, 256], replicated
- grad_scale: float32 [256], replicated
Inputs may be any that keep to these rules, and one draw needn't show every extreme that they name: `seam_links`: entry [t, s] = (t2, s2, f): side s of tile t meets side s2 of tile t2, reversed if f = 1. Sides are paired: entry [t2, s2] = (t, s, f), and no entry names its own side. `corner_links`: entry [t, k] = (t2, k2): corner k of tile t meets corner k2 of tile t2. Corners are paired: entry [t2, k2] = (t, k), and no entry names its own corner.
All inputs are finite; a program needn't handle non-finite values.
Results may differ from a plain program's by a relative error of at most 0.0063.
Values may be sent and summed in bfloat16 or wider, within the bound.
A program may use at most 64 MiB of HBM per device.

v0:
```python
import math

import jax
import jax.numpy as jnp
from jax import lax
from jax.sharding import PartitionSpec as P

INV_ROOT_TWO = 0.7071067811865476
INV_ROOT_TAU = 0.3989422804014327


def edge_strips(blocks):
    top_row = blocks[..., 0, :, :]
    right_col = blocks[..., :, -1, :]
    bottom_row = blocks[..., -1, ::-1, :]
    left_col = blocks[..., ::-1, 0, :]
    return jnp.stack([top_row, right_col, bottom_row, left_col], axis=-3)


def corner_cells(blocks):
    return jnp.stack(
        [
            blocks[..., 0, 0, :],
            blocks[..., 0, -1, :],
            blocks[..., -1, -1, :],
            blocks[..., -1, 0, :],
        ],
        axis=-2,
    )


def fetch_linked(all_strips, all_points, seam_links, corner_links):
    picked = all_strips[:, seam_links[..., 0], seam_links[..., 1]]
    reverse = (seam_links[..., 2] == 1)[None, :, :, None, None]
    strips = jnp.where(reverse, picked[..., ::-1, :], picked)
    points = all_points[:, corner_links[..., 0], corner_links[..., 1]]
    return (strips, points)


def assemble(blocks, strips, points):
    top_row = jnp.concatenate(
        [points[..., 0:1, :], strips[..., 0, :, :], points[..., 1:2, :]], axis=-2
    )
    bottom_row = jnp.concatenate(
        [points[..., 3:4, :], strips[..., 2, ::-1, :], points[..., 2:3, :]], axis=-2
    )
    left_col = strips[..., 3, ::-1, :][..., :, None, :]
    right_col = strips[..., 1, :, :][..., :, None, :]
    middle = jnp.concatenate([left_col, blocks, right_col], axis=-2)
    return jnp.concatenate([top_row[..., None, :, :], middle, bottom_row[..., None, :, :]], axis=-3)


def padded_parts(grad_padded):
    interior = grad_padded[..., 1:-1, 1:-1, :]
    top_row = grad_padded[..., 0, 1:-1, :]
    right_col = grad_padded[..., 1:-1, -1, :]
    bottom_row = grad_padded[..., -1, 1:-1, :][..., ::-1, :]
    left_col = grad_padded[..., 1:-1, 0, :][..., ::-1, :]
    strips = jnp.stack([top_row, right_col, bottom_row, left_col], axis=-3)
    points = jnp.stack(
        [
            grad_padded[..., 0, 0, :],
            grad_padded[..., 0, -1, :],
            grad_padded[..., -1, -1, :],
            grad_padded[..., -1, 0, :],
        ],
        axis=-2,
    )
    return (interior, strips, points)


def add_to_rims(target, strips, points):
    extent = target.shape[-2]
    row_ids = lax.broadcasted_iota(jnp.int32, (extent, 1, 1), 0)
    col_ids = lax.broadcasted_iota(jnp.int32, (1, extent, 1), 1)
    top_mask = row_ids == 0
    bottom_mask = row_ids == extent - 1
    left_mask = col_ids == 0
    right_mask = col_ids == extent - 1
    target = target + jnp.where(top_mask, strips[..., 0, :, :][..., None, :, :], 0.0)
    target = target + jnp.where(right_mask, strips[..., 1, :, :][..., :, None, :], 0.0)
    target = target + jnp.where(bottom_mask, strips[..., 2, ::-1, :][..., None, :, :], 0.0)
    target = target + jnp.where(left_mask, strips[..., 3, ::-1, :][..., :, None, :], 0.0)
    target = target + jnp.where(top_mask & left_mask, points[..., 0, :][..., None, None, :], 0.0)
    target = target + jnp.where(top_mask & right_mask, points[..., 1, :][..., None, None, :], 0.0)
    target = target + jnp.where(
        bottom_mask & right_mask, points[..., 2, :][..., None, None, :], 0.0
    )
    target = target + jnp.where(bottom_mask & left_mask, points[..., 3, :][..., None, None, :], 0.0)
    return target


def forward_backward(
    padded, blocks, grad_out, dw_weight, norm_gain, w_in, bias_in, w_out, layer_scale
):
    extent = blocks.shape[-2]
    channels = blocks.shape[-1]
    mixed_cells = jnp.zeros(blocks.shape, jnp.float32)
    for row_off in range(3):
        for col_off in range(3):
            tap_index = 3 * row_off + col_off
            window = padded[..., row_off : row_off + extent, col_off : col_off + extent, :].astype(
                jnp.float32
            )
            mixed_cells = mixed_cells + window * dw_weight[:, tap_index]
    average = jnp.mean(mixed_cells, axis=-1, keepdims=True)
    centred = mixed_cells - average
    inv_std = lax.rsqrt(jnp.mean(centred * centred, axis=-1, keepdims=True) + 1e-06)
    standard = centred * inv_std
    normed = (standard * norm_gain).astype(jnp.bfloat16).reshape(-1, channels)
    hidden_pre = jnp.dot(normed, w_in, preferred_element_type=jnp.float32) + bias_in
    activated = jax.nn.gelu(hidden_pre, approximate=False).astype(jnp.bfloat16)
    branch = jnp.dot(activated, w_out, preferred_element_type=jnp.float32)
    cotangent = grad_out.reshape(-1, channels).astype(jnp.float32)
    block_out = (
        (blocks.reshape(-1, channels).astype(jnp.float32) + layer_scale * branch)
        .astype(jnp.bfloat16)
        .reshape(blocks.shape)
    )
    grad_scale = jnp.sum(cotangent * branch, axis=0)
    grad_mix = (cotangent * layer_scale).astype(jnp.bfloat16)
    grad_w_out = lax.dot_general(
        activated, grad_mix, (((0,), (0,)), ((), ())), preferred_element_type=jnp.float32
    )
    grad_act = lax.dot_general(
        grad_mix, w_out, (((1,), (1,)), ((), ())), preferred_element_type=jnp.float32
    )
    gelu_slope = (
        0.5 * (1.0 + lax.erf(hidden_pre * INV_ROOT_TWO))
        + hidden_pre * jnp.exp(-0.5 * hidden_pre * hidden_pre) * INV_ROOT_TAU
    )
    grad_hidden = (grad_act * gelu_slope).astype(jnp.bfloat16)
    grad_bias = jnp.sum(grad_hidden.astype(jnp.float32), axis=0)
    grad_w_in = lax.dot_general(
        normed, grad_hidden, (((0,), (0,)), ((), ())), preferred_element_type=jnp.float32
    )
    grad_normed = lax.dot_general(
        grad_hidden, w_in, (((1,), (1,)), ((), ())), preferred_element_type=jnp.float32
    ).reshape(blocks.shape)
    grad_gain = jnp.sum((grad_normed * standard).reshape(-1, channels), axis=0)
    grad_unit = grad_normed * norm_gain
    grad_mixed = (
        grad_unit
        - jnp.mean(grad_unit, axis=-1, keepdims=True)
        - standard * jnp.mean(grad_unit * standard, axis=-1, keepdims=True)
    ) * inv_std
    pad_widths = [(0, 0)] * (grad_mixed.ndim - 3) + [(2, 2), (2, 2), (0, 0)]
    wide_grad = jnp.pad(grad_mixed, pad_widths)
    grad_padded = jnp.zeros(padded.shape, jnp.float32)
    dw_columns = []
    for row_off in range(3):
        for col_off in range(3):
            tap_index = 3 * row_off + col_off
            window = padded[..., row_off : row_off + extent, col_off : col_off + extent, :].astype(
                jnp.float32
            )
            shifted = wide_grad[
                ..., 2 - row_off : 4 - row_off + extent, 2 - col_off : 4 - col_off + extent, :
            ]
            grad_padded = grad_padded + shifted * dw_weight[:, tap_index]
            dw_columns.append(jnp.sum((grad_mixed * window).reshape(-1, channels), axis=0))
    grad_dw = jnp.stack(dw_columns, axis=1)
    return (
        block_out,
        grad_padded,
        (grad_dw, grad_gain, grad_w_in, grad_bias, grad_w_out, grad_scale),
    )


def body(
    inputs,
    grad_out,
    seam_links,
    corner_links,
    dw_weight,
    norm_gain,
    w_in,
    bias_in,
    w_out,
    layer_scale,
):
    all_strips, all_points = (
        lax.all_gather(edge_strips(inputs), "tile", axis=1, tiled=True),
        lax.all_gather(corner_cells(inputs), "tile", axis=1, tiled=True),
    )
    strips, points = fetch_linked(all_strips, all_points, seam_links, corner_links)
    padded = assemble(inputs, strips, points)
    block_out, grad_padded, partials = forward_backward(
        padded, inputs, grad_out, dw_weight, norm_gain, w_in, bias_in, w_out, layer_scale
    )
    grad_dw, grad_gain, grad_w_in, grad_bias, grad_w_out, grad_scale = partials
    interior, back_strips, back_points = padded_parts(grad_padded)
    home_strips, home_points = (
        lax.all_gather(back_strips.astype(jnp.bfloat16), "tile", axis=1, tiled=True).astype(
            back_strips.dtype
        ),
        lax.all_gather(back_points.astype(jnp.bfloat16), "tile", axis=1, tiled=True).astype(
            back_points.dtype
        ),
    )
    return_strips, return_points = fetch_linked(home_strips, home_points, seam_links, corner_links)
    x_grad = add_to_rims(grad_out.astype(jnp.float32) + interior, return_strips, return_points)
    cell_total = (
        lax.axis_size("tile")
        * lax.axis_size("rep")
        * inputs.shape[0]
        * inputs.shape[1]
        * inputs.shape[2]
        * inputs.shape[3]
    )
    factor = 1.0 / math.sqrt(cell_total)
    summed = lax.psum(
        (grad_dw, grad_gain, grad_w_in, grad_bias, grad_w_out, grad_scale), ("tile", "rep")
    )
    return (
        block_out,
        x_grad,
        summed[0] * factor,
        summed[1] * factor,
        summed[2] * factor,
        summed[3] * factor,
        summed[4] * factor,
        summed[5] * factor,
    )


def solution(mesh):
    placed = (
        P("rep", "tile", None, None, None),
        P("rep", "tile", None, None, None),
        P("tile", None, None),
        P("tile", None, None),
        P(),
        P(),
        P(),
        P(),
        P(),
        P(),
    )
    return jax.shard_map(
        body,
        mesh=mesh,
        in_specs=placed,
        out_specs=(
            P("rep", "tile", None, None, None),
            P("rep", "tile", None, None, None),
            P(),
            P(),
            P(),
            P(),
            P(),
            P(),
        ),
        check_vma=False,
    )
```

profile of v0, /device:TPU:1, one launch (start us, length us, event | category | flops | bytes accessed | tf_op | source)
XLA Modules:
  0.0 215.0 jit_solution(4268885214619424398)
XLA Ops:
  7.2 0.0 all-reduce.5.cloned.1.call-start
  7.3 0.9 fusion.76
  8.1 1.1 fusion.75
  9.3 0.8 slice_bitcast_fusion.8
  10.1 0.7 fusion.80
  10.7 0.7 compare_bitcast_fusion
  11.5 6.1 %all_gather.12 = bf16[1,8,4,256]{3,2,0,1:T(4,128)(2,1)S(1)} all-gather(bf16[1,2,4,256]{3,2,0,1:T(4,128)(2,1)S(1)} %copy.212), channel_id=1, replica_groups=mesh['tile'=4,'rep'=8] {'tile'}, dimensions={1}, use_global_device_ids=true | all-gather | bytes 20480 | tf_op jit(solution)/shard_map/all_gather | solution.py:184
  17.5 0.8 fusion.71
  18.3 0.1 reshape.476
  18.4 0.6 gather_fusion
  19.0 0.1 rev.31
  19.2 0.1 rev.30
  19.3 7.7 %all_gather.13 = bf16[1,8,4,32,256]{4,3,1,2,0:T(8,128)(2,1)S(1)} all-gather(bf16[1,2,4,32,256]{4,3,1,2,0:T(8,128)(2,1)S(1)} %pad_maximum_fusion.3), channel_id=1, replica_groups=mesh['tile'=4,'rep'=8] {'tile'}, dimensions={1}, use_global_device_ids=true | all-gather | bytes 655360 | tf_op jit(solution)/shard_map/all_gather | solution.py:183
  27.0 0.1 reshape.484
  27.1 0.6 gather_fusion.1
  27.6 0.1 rev.32
  27.8 0.1 broadcast_select_fusion.1
  27.9 0.1 rev.34
  28.0 0.1 rev.33
  28.1 0.1 copy.219
  28.1 0.1 copy.220
  28.3 1.7 maximum_maximum_fusion
  30.0 5.2 %fusion.72 = (f32[2,32,32]{2,1,0:T(8,128)S(1)}, f32[1,2,32,32,256]{4,3,2,1,0:T(8,128)S(1)}) fusion(f32[256]{0:T(256)S(1)} %bitcast.170, bf16[1,2,33,34,256]{4,3,2,1,0:T(8,128)(2,1)S(1)} %get-tuple-element.81, f32[256]{0:T(256)S(1)} %bitcast.172, f32[256]{0:T(256)S(1)} %bitcast.158, f32[256]{0:T(256)S(1)} %bitcast.160, ...), kind=kLoop, calls=%fused_computation.185 | loop fusion | flops 17299456 | bytes 9520128 | tf_op jit(solution)/shard_map/reduce_sum | solution.py:106
  35.2 0.6 multiply_reduce_fusion.4
  35.9 0.7 multiply_convert_fusion
  36.7 19.3 %fusion.2 = (bf16[2048,1024]{1,0:T(8,128)(2,1)S(1)}, f32[2048,1024]{1,0:T(8,128)S(1)}) fusion(f32[1024]{0:T(1024)S(1)} %copy-done.13, bf16[2048,256]{1,0:T(8,128)(2,1)S(1)} %bitcast.144, bf16[256,1024]{1,0:T(8,128)(2,1)S(1)} %copy-done), kind=kOutput, calls=%fused_computation.8 | convolution fusion | flops 1212153856 | bytes 14159872 | tf_op jit(solution)/shard_map/dot_general | solution.py:111
  56.1 3.1 %fusion.58 = (f32[256]{0:T(256)}, bf16[2048,256]{1,0:T(8,128)(2,1)}, bf16[2048,256]{1,0:T(8,128)(2,1)S(1)}) fusion(bf16[1,2,32,32,256]{4,3,2,1,0:T(8,128)(2,1)S(1)} %copy-done.6, f32[256]{0:T(256)S(1)} %copy-done.14, bf16[1,2,32,32,256]{4,3,2,1,0:T(8,128)(2,1)S(1)} %copy-done.5, bf16[2048,1024]{1,0:T(8,128)(2,1)S(1)} %get-tuple-element.122, ...), kind=kOutput, calls=%fused_computation.102 | convolution fusion | flops 1078460160 | bytes 8914944 | tf_op jit(solution)/shard_map/dot_general | solution.py:113
  59.2 2.2 %fusion.82 = f32[1024,256]{1,0:T(8,128)} fusion(bf16[2048,1024]{1,0:T(8,128)(2,1)S(1)} %get-tuple-element.122, bf16[2048,256]{1,0:T(8,128)(2,1)S(1)} %get-tuple-element.82), kind=kOutput, calls=%fused_computation.194 | convolution fusion | flops 1073741824 | bytes 6291456 | tf_op jit(solution)/shard_map/dot_general | solution.py:122
  61.4 4.9 %convert_reduce_fusion = (f32[1024]{0:T(1024)S(1)}, bf16[2048,1024]{1,0:T(8,128)(2,1)S(1)}) fusion(f32[2048,1024]{1,0:T(8,128)S(1)} %get-tuple-element.123, f32[1024]{0:T(1024)S(1)} %copy-done.13, bf16[2048,256]{1,0:T(8,128)(2,1)S(1)} %get-tuple-element.82, bf16[1024,256]{1,0:T(8,128)(2,1)S(1)} %copy-done.12), kind=kOutput, calls=%fused_computation.15 | convolution fusion | flops 1101003776 | bytes 14163968 | tf_op jit(solution)/shard_map/dot_general | solution.py:125
  66.3 1.9 copy-done.15
  68.3 2.2 %fusion.81 = f32[256,1024]{1,0:T(8,128)} fusion(bf16[2048,256]{1,0:T(8,128)(2,1)S(1)} %bitcast.145, bf16[2048,1024]{1,0:T(8,128)(2,1)S(1)} %get-tuple-element.127), kind=kOutput, calls=%fused_computation.193 | convolution fusion | flops 1073741824 | bytes 6291456 | tf_op jit(solution)/shard_map/dot_general | solution.py:134
  70.5 3.6 %multiply_reduce_fusion.3 = (f32[2048]{0:T(1024)S(1)}, f32[2048,256]{1,0:T(8,128)S(1)}) fusion(f32[256]{0:T(256)S(1)} %copy-done.9, bf16[2048,1024]{1,0:T(8,128)(2,1)} %copy-done.15, bf16[256,1024]{1,0:T(8,128)(2,1)S(1)} %copy-done), kind=kOutput, calls=%fused_computation.109 | convolution fusion | flops 1074788352 | bytes 6824960 | tf_op jit(solution)/shard_map/dot_general | solution.py:137
  74.1 1.1 multiply_reduce_fusion
  75.2 0.2 copy-done.3
  75.5 0.1 div.17
  75.5 8.3 %fusion.48 = (f32[256]{0:T(256)S(1)}, f32[256]{0:T(256)S(1)}, f32[256]{0:T(256)S(1)}, f32[256]{0:T(256)S(1)}, f32[256]{0:T(256)S(1)}, /*index=5*/f32[256]{0:T(25...) fusion(bf16[1,2,33,34,256]{4,3,2,1,0:T(8,128)(2,1)} %copy-done.2, ...), kind=kLoop, calls=%fused_computation.89 | loop fusion | flops 20969216 | bytes 13740032 | tf_op jit(solution)/shard_map/reduce_sum | solution.py:161
  83.9 2.8 %fusion.24 = f32[1,2,34,34,256]{4,3,2,1,0:T(8,128)S(1)} fusion(f32[1,2,32,32,256]{4,3,2,1,0:T(8,128)S(1)} %get-tuple-element.71, f32[256]{0:T(256)S(1)} %bitcast.171, f32[256]{0:T(256)S(1)} %bitcast.173, f32[256]{0:T(256)S(1)} %bitcast.159, f32[256]{0:T(256)S(1)} %bitcast.161, f32[256]{0:T(256)S(1)} %bitcast.163, f32[256]{0:T(256)S(1)} %bitcast.165, ...), kind=kLoop, calls=%fused_computation.48 | loop fusion | flops 10061824 | bytes 4473856 | tf_op jit(solution)/shard_map/add | solution.py:160
  86.6 0.7 copy.267
  87.3 0.6 slice_bitcast_fusion.4
  88.0 0.6 fusion.74
  88.6 40.8 %all-reduce.1 = (f32[256,9]{0,1:T(8,128)}, f32[256]{0:T(256)S(1)}, f32[1024]{0:T(1024)S(1)}, f32[256]{0:T(256)S(1)}) all-reduce(f32[256,9]{0,1:T(8,128)S(1)} %stack.78, f32[256]{0:T(256)S(1)} %get-tuple-element.57, f32[1024]{0:T(1024)S(1)} %get-tuple-element.126, ...), channel_id=1, replica_groups=mesh['tile'=4,'rep'=8] {'tile','rep'}, use_global_device_ids=true, to_apply=%region_13.14 | all-reduce | flops 3840 | bytes 30720 | tf_op jit(solution)/shard_map/psum | solution.py:212
  129.4 0.6 broadcast_multiply_fusion.6
  130.0 0.6 broadcast_multiply_fusion.7
  130.6 0.6 broadcast_multiply_fusion.8
  131.1 0.1 rev.41
  131.2 0.1 rev.35
  131.3 0.8 pad_maximum_fusion.4
  132.1 8.7 %all_gather.14 = bf16[1,8,4,32,256]{4,3,2,0,1:T(8,128)(2,1)S(1)} all-gather(bf16[1,2,4,32,256]{4,3,2,0,1:T(8,128)(2,1)S(1)} %copy.228), channel_id=1, replica_groups=mesh['tile'=4,'rep'=8] {'tile'}, dimensions={1}, use_global_device_ids=true | all-gather | bytes 655360 | tf_op jit(solution)/shard_map/all_gather | solution.py:194
  140.8 1.1 bitcast_convert_fusion
  141.9 2.5 %gather_fusion.2 = f32[8,32,256]{2,1,0:T(8,128)} fusion(f32[8,4,32,256]{3,2,1,0:T(8,128)} %bitcast_convert_fusion, s32[8]{0:T(128)S(1)} %reshape.484), kind=kCustom, calls=%fused_computation.2 | custom fusion | bytes 524352 | tf_op jit(solution)/shard_map/gather | solution.py:33
  144.4 1.6 rev.37
  146.0 1.1 broadcast_select_fusion
  147.1 0.7 slice_bitcast_fusion.1
  147.8 0.7 copy.274
  148.5 5.1 %all_gather.15 = bf16[1,8,4,256]{3,2,0,1:T(4,128)(2,1)S(1)} all-gather(bf16[1,2,4,256]{3,2,0,1:T(4,128)(2,1)S(1)} %copy.230), channel_id=1, replica_groups=mesh['tile'=4,'rep'=8] {'tile'}, dimensions={1}, use_global_device_ids=true | all-gather | bytes 20480 | tf_op jit(solution)/shard_map/all_gather | solution.py:197
  153.7 0.6 gather_fusion.3
  154.3 0.1 rev.38
  154.3 0.8 rev.39
  155.2 0.1 broadcast_and_fusion.1
  155.3 0.6 broadcast_multiply_fusion.4
  155.9 4.5 %fusion.56 = f32[1,2,32,32,256]{4,3,2,1,0:T(8,128)} fusion(f32[1,2,34,34,256]{4,3,2,1,0:T(8,128)S(1)} %fusion.24, bf16[1,2,32,32,256]{4,3,2,1,0:T(8,128)(2,1)} %param.11, f32[2,256]{1,0:T(2,128)S(1)} %bitcast.174, f32[2,256]{1,0:T(2,128)S(1)} %bitcast.175, f32[2,256]{1,0:T(2,128)S(1)} %bitcast.176, f32[2,256]{1,0:T(2,128)S(1)} %bitcast.177, ...), kind=kLoop, calls=%fused_computation.98 | loop fusion | flops 9437184 | bytes 5531648 | tf_op jit(solution)/shard_map/add | solution.py:89
  160.3 44.4 %all-reduce.5.cloned.1.call-done = (f32[256,1024]{1,0:T(8,128)}, f32[1024,256]{1,0:T(8,128)}) async-done(((f32[256,1024]{1,0:T(8,128)}, f32[1024,256]{1,0:T(8,128)}), (f32[256,1024]{1,0:T(8,128)}, f32[1024,256]{1,0:T(8,128)})) %all-reduce.5.cloned.1.call-update) | async-done | bytes 2097168 | tf_op jit(solution)/shard_map/psum | solution.py:212
  204.7 2.4 %broadcast_multiply_fusion = f32[1024,256]{1,0:T(8,128)} fusion(f32[1024,256]{1,0:T(8,128)} %get-tuple-element.70), kind=kLoop, calls=%fused_computation.118 | loop fusion | flops 262144 | bytes 2097152 | tf_op jit(solution)/shard_map/mul | solution.py:222
  207.1 1.1 broadcast_multiply_fusion.1
  (69 shorter events, 0.5 us)
Async XLA Ops:
  7.2 29.5 %copy-start = (bf16[256,1024]{1,0:T(8,128)(2,1)S(1)}, bf16[256,1024]{1,0:T(8,128)(2,1)}, u32[]{:S(2)}) copy-start(bf16[256,1024]{1,0:T(8,128)(2,1)} %param.16) | copy-start | bytes 1572868
  7.2 21.1 %copy-start.4 = (bf16[1,2,32,32,256]{4,3,2,1,0:T(8,128)(2,1)S(1)}, bf16[1,2,32,32,256]{4,3,2,1,0:T(8,128)(2,1)}, u32[]{:S(2)}) copy-start(bf16[1,2,32,32,256]{4,3,2,1,0:T(8,128)(2,1)} %param.10) | copy-start | bytes 3145732
  7.2 21.0 %copy-start.10 = (f32[256,9]{0,1:T(8,128)S(1)}, f32[256,9]{0,1:T(8,128)}, u32[]{:S(2)}) copy-start(f32[256,9]{0,1:T(8,128)} %param.14) | copy-start | bytes 27652
  7.2 197.5 %all-reduce.5.cloned.1.call-start = ((), (), s32[]{:S(2)}) async-start(), calls=%async_computation | async-start | bytes 4194304 | tf_op jit(solution)/shard_map/psum | solution.py:212
  11.4 16.3 %copy-start.11 = (pred[2,4]{1,0:T(4,128)(4,1)}, pred[2,4]{1,0:T(4,128)(4,1)S(1)}, u32[]{:S(2)}) copy-start(pred[2,4]{1,0:T(4,128)(4,1)S(1)} %compare_bitcast_fusion) | copy-start | bytes 28
  30.0 5.2 %copy-start.1 = (bf16[1,2,33,34,256]{4,3,2,1,0:T(8,128)(2,1)}, bf16[1,2,33,34,256]{4,3,2,1,0:T(8,128)(2,1)S(1)}, u32[]{:S(2)}) copy-start(bf16[1,2,33,34,256]{4,3,2,1,0:T(8,128)(2,1)S(1)} %get-tuple-element.80) | copy-start | bytes 3446788
  30.0 5.2 %copy-start.2 = (bf16[1,2,33,34,256]{4,3,2,1,0:T(8,128)(2,1)}, bf16[1,2,33,34,256]{4,3,2,1,0:T(8,128)(2,1)S(1)}, u32[]{:S(2)}) copy-start(bf16[1,2,33,34,256]{4,3,2,1,0:T(8,128)(2,1)S(1)} %get-tuple-element.81) | copy-start | bytes 3446788
  30.0 5.9 %copy-start.9 = (f32[256]{0:T(256)S(1)}, f32[256]{0:T(256)}, u32[]{:S(2)}) copy-start(f32[256]{0:T(256)} %param.15) | copy-start | bytes 3076
  35.2 1.4 copy-start.13
  36.7 19.4 %copy-start.5 = (bf16[1,2,32,32,256]{4,3,2,1,0:T(8,128)(2,1)S(1)}, bf16[1,2,32,32,256]{4,3,2,1,0:T(8,128)(2,1)}, u32[]{:S(2)}) copy-start(bf16[1,2,32,32,256]{4,3,2,1,0:T(8,128)(2,1)} %param.10) | copy-start | bytes 3145732
  36.7 19.4 %copy-start.6 = (bf16[1,2,32,32,256]{4,3,2,1,0:T(8,128)(2,1)S(1)}, bf16[1,2,32,32,256]{4,3,2,1,0:T(8,128)(2,1)}, u32[]{:S(2)}) copy-start(bf16[1,2,32,32,256]{4,3,2,1,0:T(8,128)(2,1)} %param.11) | copy-start | bytes 3145732
  36.7 19.4 %copy-start.12 = (bf16[1024,256]{1,0:T(8,128)(2,1)S(1)}, bf16[1024,256]{1,0:T(8,128)(2,1)}, u32[]{:S(2)}) copy-start(bf16[1024,256]{1,0:T(8,128)(2,1)} %param.18) | copy-start | bytes 1572868
  36.7 19.4 %copy-start.14 = (f32[256]{0:T(256)S(1)}, f32[256]{0:T(256)}, u32[]{:S(2)}) copy-start(f32[256]{0:T(256)} %param.19) | copy-start | bytes 3076
  66.3 1.9 copy-start.15
  74.1 1.3 copy-start.3
  132.1 23.1 %copy-start.8 = (f32[256,9]{0,1:T(8,128)S(1)}, f32[256,9]{0,1:T(8,128)}, u32[]{:S(2)}) copy-start(f32[256,9]{0,1:T(8,128)} %get-tuple-element.65) | copy-start | bytes 27652
  204.7 2.4 %copy-start.7 = (f32[256,1024]{1,0:T(8,128)S(1)}, f32[256,1024]{1,0:T(8,128)}, u32[]{:S(2)}) copy-start(f32[256,1024]{1,0:T(8,128)} %get-tuple-element.69) | copy-start | bytes 3145732
Sparse Core Ops, SparseCore 0:
  70.6 134.0 all-reduce.4
where the time goes:
time: 217 us; the launch traced here: 215 us
  blocking collectives  68.3 us (31%)
  waiting for transfers between devices  44.4 us (20%)
  other arithmetic  35.4 us (16%)
  matrix products  35.4 us (16%)
  local copies, waits for them, and re-layouts  16.8 us (8%)
  between operations  14.6 us (7%)
    psum x1, waiting for transfers between devices, body(): lax.psum((grad_dw, grad_gain, grad_w_in, grad_bias, grad_w_out, grad_scal...  44.4 us
    psum x1, blocking collectives, body(): lax.psum((grad_dw, grad_gain, grad_w_in, grad_bias, grad_w_out, grad_scal...  40.8 us
    dot_general x1, matrix products, forward_backward(): jnp.dot(normed, w_in, preferred_element_type=jnp.float32) + bias_in  19.3 us
    all_gather x1, blocking collectives, body(): lax.all_gather(back_strips.astype(jnp.bfloat16), 'tile', axis=1, tiled=True)  8.66 us
    reduce_sum x1, other arithmetic, forward_backward(): jnp.sum((grad_mixed * window).reshape(-1, channels), axis=0)  8.32 us
    all_gather x1, blocking collectives, body(): lax.all_gather(edge_strips(inputs), 'tile', axis=1, tiled=True)  7.66 us
    all_gather x1, blocking collectives, body(): lax.all_gather(corner_cells(inputs), 'tile', axis=1, tiled=True)  6.07 us
    reduce_sum x1, other arithmetic, forward_backward(): average = jnp.mean(mixed_cells, axis=-1, keepdims=True)  5.16 us
  transfers between devices with their start and end apart: 1, of which 1 were waited for; matrix products, arithmetic and copies ran while one was open for 16% of the time, Pallas kernels for 0%

commit v1 on v0

v1 whole, which is shorter than its diff:
```python
import functools
import math

import jax
import jax.numpy as jnp
from jax import lax
from jax.experimental import pallas as pl
from jax.experimental.pallas import tpu as pltpu
from jax.sharding import PartitionSpec as P

INV_ROOT_TWO = 0.7071067811865476
INV_ROOT_TAU = 0.3989422804014327
MESH = pl.DeviceIdType.MESH
F32 = jnp.float32
BF16 = jnp.bfloat16
VMEM = pl.BlockSpec(memory_space=pltpu.VMEM)
SMEM = pl.BlockSpec(memory_space=pltpu.SMEM)
NN = (((1,), (0,)), ((), ()))
NT = (((1,), (1,)), ((), ()))
TN = (((0,), (0,)), ((), ()))
SIDES = 4
CORNER_ROWS = 16


def dot(a, b, dims=NN):
    return lax.dot_general(a, b, dims, preferred_element_type=F32)


def iota(shape, dim):
    return lax.broadcasted_iota(jnp.int32, shape, dim)


def one_hot(mask):
    return jnp.where(mask, 1.0, 0.0).astype(BF16)


def tile_gather(tiles, buf, send_sem, recv_sem):
    size = lax.axis_size("tile")
    me = lax.axis_index("tile")
    mine = pl.ds(me * tiles, tiles)
    copies = []
    for k in range(1, size):
        copy = pltpu.make_async_remote_copy(
            src_ref=buf.at[mine],
            dst_ref=buf.at[mine],
            send_sem=send_sem.at[k - 1],
            recv_sem=recv_sem.at[k - 1],
            device_id={"tile": lax.rem(me + k, size)},
            device_id_type=MESH,
        )
        copy.start()
        copies.append(copy)
    return copies


def halo_kernel(side, tiles, x_ref, out_ref, land, send_sem, recv_sem):
    size = lax.axis_size("tile")
    me = lax.axis_index("tile")
    barrier = pltpu.get_barrier_semaphore()
    for k in range(1, size):
        pl.semaphore_signal(
            barrier, inc=1, device_id={"tile": lax.rem(me + k, size)}, device_id_type=MESH
        )
    rows = SIDES * side
    cells = side * side
    r = iota((rows, cells), 0)
    c = iota((rows, cells), 1)
    s = r // side
    p = r % side
    target = jnp.where(
        s == 0,
        p,
        jnp.where(
            s == 1,
            p * side + side - 1,
            jnp.where(s == 2, (side - 1) * side + p, p * side),
        ),
    )
    sel = one_hot(c == target)
    for t in range(tiles):
        land[me * tiles + t] = dot(sel, x_ref[t]).astype(BF16)
    pl.semaphore_wait(barrier, size - 1)
    copies = tile_gather(tiles, land, send_sem, recv_sem)
    for copy in copies:
        copy.wait()
    out_ref[...] = land[...]


def gather_halos(x):
    tiles, cells, channels = x.shape
    side = math.isqrt(cells)
    size = lax.axis_size("tile")
    shape = (size * tiles, SIDES * side, channels)
    return pl.pallas_call(
        functools.partial(halo_kernel, side, tiles),
        out_shape=jax.ShapeDtypeStruct(shape, BF16),
        in_specs=[VMEM],
        out_specs=VMEM,
        scratch_shapes=[
            pltpu.VMEM(shape, BF16),
            pltpu.SemaphoreType.DMA((size - 1,)),
            pltpu.SemaphoreType.DMA((size - 1,)),
        ],
        compiler_params=pltpu.CompilerParams(
            collective_id=0, has_side_effects=True, vmem_limit_bytes=32 * 2**20
        ),
        name="halo_gather",
    )(x)


def compute_kernel(
    side,
    tiles,
    seam_ref,
    corner_ref,
    strips_ref,
    x_ref,
    g_ref,
    dw_ref,
    gain_ref,
    w_in_ref,
    bias_ref,
    w_out_ref,
    scale_ref,
    out_ref,
    xg_ref,
    back_ref,
    acc_ref,
    small_ref,
    xs,
    gm_buf,
    strip_buf,
    dw_acc,
    vec_acc,
    bias_acc,
):
    channels = x_ref.shape[-1]
    hidden = w_in_ref.shape[1]
    ext = side + 2
    last = side - 1
    gain = gain_ref[...]
    scale = scale_ref[...]
    chunk_rows = 8
    n = chunk_rows * side
    hb = 256
    lanes = 128

    dw_acc[...] = jnp.zeros_like(dw_acc)
    vec_acc[...] = jnp.zeros_like(vec_acc)
    bias_acc[...] = jnp.zeros_like(bias_acc)
    acc_ref[...] = jnp.zeros_like(acc_ref)
    small_ref[...] = jnp.zeros_like(small_ref)
    strip_buf[...] = jnp.zeros_like(strip_buf)

    for t in range(tiles):
        picks = []
        flips = []
        for s in range(SIDES):
            t2, s2, f = seam_ref[t, s, 0], seam_ref[t, s, 1], seam_ref[t, s, 2]
            flip = lax.rem(f + (1 if s >= 2 else 0) + jnp.where(s2 >= 2, 1, 0), 2)
            picks.append(strips_ref[t2, pl.ds(pl.multiple_of(s2 * side, side), side), :])
            flips.append(flip)
        corner_rows = []
        for k in range(4):
            t2, k2 = corner_ref[t, k, 0], corner_ref[t, k, 1]
            picks.append(strips_ref[t2, pl.ds(pl.multiple_of(k2 * side, side), side), :])
            corner_rows.append(jnp.where(k2 >= 2, last, 0))
        table = jnp.concatenate(picks, axis=0)

        def place(p, s):
            return s * side + p + flips[s] * (last - 2 * p)

        def corner_place(k):
            return SIDES * side + k * side + corner_rows[k]

        p = iota((side, 2 * SIDES * side), 0)
        r = iota((side, 2 * SIDES * side), 1)
        xs[1, t, 0:side, :] = dot(one_hot(r == place(p, 0)), table)
        xs[1, t, (ext - 1) * side :, :] = dot(one_hot(r == place(p, 2)), table)
        xs[1, t, side : (ext - 1) * side, :] = x_ref[t].astype(F32)
        half = ext // 2 * side

        def shift_rows(h, _, t=t):
            start = pl.multiple_of(h * half, side)
            rows = xs[1, t, pl.ds(start, half), :]
            cell = start + iota((half, 1), 0)
            i = cell // side - 1
            j = cell % side
            rr = iota((half, 2 * SIDES * side), 1)

            def column(sd, k_top, k_bottom):
                return jnp.where(
                    i < 0,
                    corner_place(k_top),
                    jnp.where(i > last, corner_place(k_bottom), place(i, sd)),
                )

            left = jnp.where(j == 0, column(3, 0, 3), -1)
            right = jnp.where(j == last, column(1, 1, 2), -1)
            ins_left = dot(one_hot(rr == left), table)
            ins_right = dot(one_hot(rr == right), table)
            xs[0, t, pl.ds(start, half), :] = jnp.where(j == 0, ins_left, pltpu.roll(rows, 1, 0))
            xs[2, t, pl.ds(start, half), :] = jnp.where(
                j == last, ins_right, pltpu.roll(rows, half - 1, 0)
            )
            return 0

        lax.fori_loop(0, 2, shift_rows, 0)
        gm_buf[t, 0:side, :] = jnp.zeros((side, channels), F32)
        gm_buf[t, (ext - 1) * side :, :] = jnp.zeros((side, channels), F32)

    chunks = side // chunk_rows

    def fold(v):
        return jnp.sum(v.reshape(v.shape[0] // 8, 8, v.shape[1]), axis=0)

    def step(idx, _):
        t = idx // chunks
        base = pl.multiple_of(lax.rem(idx, chunks) * n, n)
        mixed = jnp.zeros((n, channels), F32)
        for a in range(3):
            for b in range(3):
                w = dw_ref[3 * a + b : 3 * a + b + 1, :]
                mixed = mixed + xs[b, t, pl.ds(base + a * side, n), :] * w
        mean = jnp.mean(mixed, axis=-1, keepdims=True)
        centred = mixed - mean
        inv_std = lax.rsqrt(jnp.mean(centred * centred, axis=-1, keepdims=True) + 1e-06)
        unit = centred * inv_std
        normed = (unit * gain).astype(BF16)
        g = g_ref[t, pl.ds(base, n), :].astype(F32)
        mix = (g * scale).astype(BF16)
        branch = jnp.zeros((n, channels), F32)
        gn = jnp.zeros((n, channels), F32)
        for h in range(hidden // hb):
            cols = slice(h * hb, (h + 1) * hb)
            pre = dot(normed, w_in_ref[:, cols]) + bias_ref[:, cols]
            phi_cum = 0.5 * (1.0 + lax.erf(pre * INV_ROOT_TWO))
            act = (pre * phi_cum).astype(BF16)
            slope = phi_cum + pre * jnp.exp(-0.5 * pre * pre) * INV_ROOT_TAU
            gact = dot(mix, w_out_ref[cols, :], NT)
            ghf = (gact * slope).astype(BF16)
            branch = branch + dot(act, w_out_ref[cols, :])
            gn = gn + dot(ghf, w_in_ref[:, cols], NT)
            bias_acc[:, cols] += fold(ghf.astype(F32))
            gwi = dot(normed, ghf, TN)
            gwo = dot(mix, act, TN)
            for q in range(hb // lanes):
                blk = h * (hb // lanes) + q
                acc_ref[blk] += gwi[:, q * lanes : (q + 1) * lanes]
                acc_ref[hidden // lanes + blk] += gwo[:, q * lanes : (q + 1) * lanes]
        x = x_ref[t, pl.ds(base, n), :].astype(F32)
        out_ref[t, pl.ds(base, n), :] = (x + scale * branch).astype(BF16)
        vec_acc[0] += fold(gn * unit)
        vec_acc[1] += fold(g * branch)
        u = gn * gain
        gm = (
            u
            - jnp.mean(u, axis=-1, keepdims=True)
            - unit * jnp.mean(u * unit, axis=-1, keepdims=True)
        ) * inv_std
        gm_buf[t, pl.ds(base + side, n), :] = gm
        for a in range(3):
            for b in range(3):
                dw_acc[3 * a + b] += fold(gm * xs[b, t, pl.ds(base + a * side, n), :])
        return 0

    lax.fori_loop(0, tiles * chunks, step, 0)

    def taps(t, start, size, b):
        total = jnp.zeros((size, channels), F32)
        for a in range(3):
            w = dw_ref[3 * a + b : 3 * a + b + 1, :]
            total = total + gm_buf[t, pl.ds(start + (2 - a) * side, size), :] * w
        return total

    def back_step(idx, _):
        t = idx // chunks
        c = lax.rem(idx, chunks)
        base = pl.multiple_of(c * n, n)
        j = iota((n, 1), 0) % side
        left = taps(t, base, n, 0)
        right = taps(t, base, n, 2)
        grad = g_ref[t, pl.ds(base, n), :].astype(F32) + taps(t, base, n, 1)
        grad = grad + jnp.where(j == last, 0.0, pltpu.roll(left, n - 1, 0))
        grad = grad + jnp.where(j == 0, 0.0, pltpu.roll(right, 1, 0))
        xg_ref[t, pl.ds(base, n), :] = grad
        ri = iota((chunk_rows, n), 0)
        ci = iota((chunk_rows, n), 1)
        row0 = pl.multiple_of(c * chunk_rows, chunk_rows)
        strip_buf[t, pl.ds(3 * side + row0, chunk_rows), :] = dot(
            one_hot(ci == ri * side), left.astype(BF16)
        )
        strip_buf[t, pl.ds(side + row0, chunk_rows), :] = dot(
            one_hot(ci == ri * side + last), right.astype(BF16)
        )
        return 0

    lax.fori_loop(0, tiles * chunks, back_step, 0)
    j = iota((side, 1), 0)
    for t in range(tiles):
        for s, a, row in ((0, 0, 1), (2, 2, side)):
            edge = gm_buf[t, row * side : (row + 1) * side, :]
            left = edge * dw_ref[3 * a : 3 * a + 1, :]
            mid = edge * dw_ref[3 * a + 1 : 3 * a + 2, :]
            right = edge * dw_ref[3 * a + 2 : 3 * a + 3, :]
            mid = mid + jnp.where(j == last, 0.0, pltpu.roll(left, side - 1, 0))
            mid = mid + jnp.where(j == 0, 0.0, pltpu.roll(right, 1, 0))
            strip_buf[t, s * side : (s + 1) * side, :] = mid
            k_left, k_right = (0, 1) if s == 0 else (3, 2)
            at = SIDES * side
            strip_buf[t, at + k_left : at + k_left + 1, :] = left[0:1, :]
            strip_buf[t, at + k_right : at + k_right + 1, :] = right[last : last + 1, :]
    back_ref[...] = strip_buf[...].astype(BF16)
    for k in range(9):
        small_ref[k : k + 1, :] = jnp.sum(dw_acc[k], axis=0, keepdims=True)
    for k in range(2):
        small_ref[9 + k : 10 + k, :] = jnp.sum(vec_acc[k], axis=0, keepdims=True)
    for k in range(hidden // channels):
        small_ref[11 + k : 12 + k, :] = jnp.sum(
            bias_acc[:, k * channels : (k + 1) * channels], axis=0, keepdims=True
        )


def compute(seam, corner, strips, x, g, dw, gain, w_in, bias, w_out, scale):
    tiles, cells, channels = x.shape
    side = math.isqrt(cells)
    hidden = w_in.shape[1]
    ext = side + 2
    return pl.pallas_call(
        functools.partial(compute_kernel, side, tiles),
        out_shape=(
            jax.ShapeDtypeStruct(x.shape, BF16),
            jax.ShapeDtypeStruct(x.shape, F32),
            jax.ShapeDtypeStruct((tiles, SIDES * side + CORNER_ROWS, channels), BF16),
            jax.ShapeDtypeStruct((2 * hidden // 128, channels, 128), F32),
            jax.ShapeDtypeStruct((16, channels), F32),
        ),
        in_specs=[SMEM, SMEM] + [VMEM] * 9,
        out_specs=(VMEM,) * 5,
        scratch_shapes=[
            pltpu.VMEM((3, tiles, ext * side, channels), F32),
            pltpu.VMEM((tiles, ext * side, channels), F32),
            pltpu.VMEM((tiles, SIDES * side + CORNER_ROWS, channels), F32),
            pltpu.VMEM((9, 8, channels), F32),
            pltpu.VMEM((2, 8, channels), F32),
            pltpu.VMEM((8, hidden), F32),
        ],
        compiler_params=pltpu.CompilerParams(vmem_limit_bytes=50 * 2**20),
        name="block_grads",
    )(seam, corner, strips, x, g, dw, gain, w_in, bias, w_out, scale)


def digits_of(tile_size, rep_size):
    low = 2 ** (int(math.log2(rep_size)) // 2)
    core = ("tile", 1, 2)
    rest = ("tile", 2, tile_size // 2)
    near = ("rep", 1, low)
    far = ("rep", low, rep_size // low)
    return core, rest, near, far


def finish_kernel(
    side,
    tiles,
    factor,
    orders,
    seam_ref,
    corner_ref,
    xg_in,
    back_ref,
    acc_ref,
    small_ref,
    xg_ref,
    gwi_ref,
    gwo_ref,
    tot_ref,
    land,
    cur,
    snd,
    rcv,
    full,
    small_slots,
    halo_send,
    halo_recv,
    rs_send,
    rs_recv,
    ag_send,
    ag_recv,
    sm_send,
    sm_recv,
):
    tile_size = lax.axis_size("tile")
    rep_size = lax.axis_size("rep")
    index = {"tile": lax.axis_index("tile"), "rep": lax.axis_index("rep")}
    core, rest, near, far = digits_of(tile_size, rep_size)
    pieces = acc_ref.shape[0]
    part_size = pieces // len(orders)
    last = side - 1

    def digit(d):
        axis, stride, size = d
        return lax.rem(index[axis] // stride, size)

    def peer(d, value):
        axis, stride, size = d
        return {axis: index[axis] + (value - digit(d)) * stride}

    barrier = pltpu.get_barrier_semaphore()
    signals = 0
    for k in range(1, tile_size):
        pl.semaphore_signal(
            barrier,
            inc=1,
            device_id={"tile": lax.rem(index["tile"] + k, tile_size)},
            device_id_type=MESH,
        )
        signals += 1
    for d in (near, far):
        for k in range(1, d[2]):
            pl.semaphore_signal(
                barrier,
                inc=1,
                device_id=peer(d, lax.rem(digit(d) + k, d[2])),
                device_id_type=MESH,
            )
            signals += 1
    pl.semaphore_wait(barrier, signals)

    land[pl.ds(index["tile"] * tiles, tiles)] = back_ref[...]

    offsets = []
    for part, order in enumerate(orders):
        off = part * part_size
        size = part_size
        stages = []
        for d in order:
            size = size // d[2]
            stages.append((off, size))
            off = off + digit(d) * size
        stages.append((off, size))
        offsets.append(stages)
    sem_at = {}
    rcv_at = {}
    sems = 0
    rows = 0
    for part, order in enumerate(orders):
        for s, d in enumerate(order):
            sem_at[part, s] = sems
            rcv_at[part, s] = rows
            sems += d[2] - 1
            rows += (d[2] - 1) * offsets[part][s][1]

    def start_scatter(part, s):
        d = orders[part][s]
        off, size = offsets[part][s]
        src = acc_ref if s == 0 else cur
        copies = []
        for k in range(1, d[2]):
            to = lax.rem(digit(d) + k, d[2])
            where = pl.ds(off + to * size, size)
            snd[where] = src[where].astype(BF16)
            copy = pltpu.make_async_remote_copy(
                src_ref=snd.at[where],
                dst_ref=rcv.at[pl.ds(rcv_at[part, s] + (k - 1) * size, size)],
                send_sem=rs_send.at[sem_at[part, s] + k - 1],
                recv_sem=rs_recv.at[sem_at[part, s] + k - 1],
                device_id=peer(d, to),
                device_id_type=MESH,
            )
            copy.start()
            copies.append(copy)
        return copies

    def end_scatter(part, s, copies):
        d = orders[part][s]
        _, size = offsets[part][s]
        off, _ = offsets[part][s + 1]
        src = acc_ref if s == 0 else cur
        total = src[pl.ds(off, size)]
        for k, copy in enumerate(copies):
            copy.wait_recv()
            total = total + rcv[pl.ds(rcv_at[part, s] + k * size, size)].astype(F32)
        if s == len(orders[part]) - 1:
            full[pl.ds(off, size)] = (total * factor).astype(BF16)
        else:
            cur[pl.ds(off, size)] = total

    def start_gather(part, s):
        d = orders[part][s]
        off, size = offsets[part][s + 1][0], offsets[part][s][1]
        copies = []
        for k in range(1, d[2]):
            to = lax.rem(digit(d) + k, d[2])
            copy = pltpu.make_async_remote_copy(
                src_ref=full.at[pl.ds(off, size)],
                dst_ref=full.at[pl.ds(off, size)],
                send_sem=ag_send.at[sem_at[part, s] + k - 1],
                recv_sem=ag_recv.at[sem_at[part, s] + k - 1],
                device_id=peer(d, to),
                device_id_type=MESH,
            )
            copy.start()
            copies.append(copy)
        return copies

    small_order = orders[0]
    small_base = [0]
    small_sem = [0]
    for d in small_order:
        small_base.append(small_base[-1] + d[2])
        small_sem.append(small_sem[-1] + d[2] - 1)

    def start_small(s, value):
        d = small_order[s]
        mine = small_base[s] + digit(d)
        small_slots[mine] = value
        copies = []
        for k in range(1, d[2]):
            to = lax.rem(digit(d) + k, d[2])
            copy = pltpu.make_async_remote_copy(
                src_ref=small_slots.at[mine],
                dst_ref=small_slots.at[mine],
                send_sem=sm_send.at[small_sem[s] + k - 1],
                recv_sem=sm_recv.at[small_sem[s] + k - 1],
                device_id=peer(d, to),
                device_id_type=MESH,
            )
            copy.start()
            copies.append(copy)
        return copies

    def end_small(s, copies):
        for copy in copies:
            copy.wait_recv()
        total = small_slots[small_base[s]]
        for k in range(1, small_order[s][2]):
            total = total + small_slots[small_base[s] + k]
        return total

    every = []
    stage_count = len(small_order)
    part_ids = range(len(orders))
    flying = {}
    for part in part_ids:
        flying[part] = start_scatter(part, 0)
        every += flying[part]
    halo = tile_gather(tiles, land, halo_send, halo_recv)
    small = start_small(0, small_ref[...])
    every += small
    for s in range(stage_count):
        for part in part_ids:
            end_scatter(part, s, flying[part])
            if s + 1 < stage_count:
                flying[part] = start_scatter(part, s + 1)
            else:
                flying[part] = start_gather(part, s)
            every += flying[part]
        value = end_small(s, small)
        if s + 1 < stage_count:
            small = start_small(s + 1, value)
            every += small
    tot_ref[...] = value * factor

    for copy in halo:
        copy.wait()
    cells = side * side
    width = SIDES * side + CORNER_ROWS
    total_rows = land.shape[0] * width
    home = land[...].reshape(total_rows, land.shape[2])
    row = iota((width, 1), 0)
    rr = iota((width, total_rows), 1)
    cell = iota((cells, 1), 0)
    i = cell // side
    j = cell % side
    r = iota((cells, width), 1)
    rim = None
    for s, (on, p) in enumerate(((i == 0, j), (j == last, i), (i == last, j), (j == 0, i))):
        hit = r == jnp.where(on, s * side + p, -1)
        rim = hit if rim is None else rim | hit
    for k, cell_k in enumerate((0, last, cells - 1, cells - side)):
        rim = rim | (r == jnp.where(cell == cell_k, SIDES * side + k, -1))
    rim = one_hot(rim)
    for t in range(tiles):
        source = jnp.full((width, 1), -1, jnp.int32)
        for s in range(SIDES):
            t2, s2, f = seam_ref[t, s, 0], seam_ref[t, s, 1], seam_ref[t, s, 2]
            flip = f + (1 if s >= 2 else 0) + s2 // 2
            flip = flip - 2 * (flip // 2)
            p = row - s * side
            at = t2 * width + s2 * side + p + flip * (last - 2 * p)
            source = jnp.where((row >= s * side) & (row < (s + 1) * side), at, source)
        for k in range(4):
            t2, k2 = corner_ref[t, k, 0], corner_ref[t, k, 1]
            at = t2 * width + SIDES * side + k2
            source = jnp.where(row == SIDES * side + k, at, source)
        table = dot(one_hot(rr == source), home).astype(BF16)
        xg_ref[t] = xg_in[t] + dot(rim, table)

    for s in reversed(range(stage_count)):
        for part in part_ids:
            for copy in flying[part]:
                copy.wait_recv()
            if s > 0:
                flying[part] = start_gather(part, s - 1)
                every += flying[part]
    channels = gwi_ref.shape[0]
    hidden = gwi_ref.shape[1]
    per = channels // 16
    for h in range(hidden // 128):
        block = full[pl.ds(h * per, per)].astype(F32).reshape(channels, 128)
        gwi_ref[:, h * 128 : (h + 1) * 128] = block
        at = (hidden // 128 + h) * per
        block = full[pl.ds(at, per)].astype(F32).reshape(channels, 128)
        gwo_ref[h * 128 : (h + 1) * 128, :] = block.T
    for copy in every:
        copy.wait_send()


def finish(seam, corner, xg, back, acc, small, factor):
    tiles, cells, channels = xg.shape
    side = math.isqrt(cells)
    tile_size = lax.axis_size("tile")
    rep_size = lax.axis_size("rep")
    acc = acc.reshape(-1, 16, 128)
    hidden = acc.shape[0] * 16 * 128 // (2 * channels)
    core, rest, near, far = digits_of(tile_size, rep_size)
    orders = [(core, rest, near, far), (core, near, rest, far)]
    if acc.shape[0] < 2 * tile_size * rep_size:
        orders = orders[:1]
    sems = 0
    rows = 0
    for order in orders:
        size = acc.shape[0] // len(orders)
        for d in order:
            size = size // d[2]
            sems += d[2] - 1
            rows += (d[2] - 1) * size
    slots = sum(d[2] for d in orders[0])
    dma = pltpu.SemaphoreType.DMA
    return pl.pallas_call(
        functools.partial(finish_kernel, side, tiles, factor, orders),
        out_shape=(
            jax.ShapeDtypeStruct(xg.shape, F32),
            jax.ShapeDtypeStruct((channels, hidden), F32),
            jax.ShapeDtypeStruct((hidden, channels), F32),
            jax.ShapeDtypeStruct(small.shape, F32),
        ),
        in_specs=[SMEM, SMEM] + [VMEM] * 4,
        out_specs=(VMEM,) * 4,
        scratch_shapes=[
            pltpu.VMEM((tile_size * tiles,) + back.shape[1:], BF16),
            pltpu.VMEM(acc.shape, F32),
            pltpu.VMEM(acc.shape, BF16),
            pltpu.VMEM((rows, 16, 128), BF16),
            pltpu.VMEM(acc.shape, BF16),
            pltpu.VMEM((slots,) + small.shape, F32),
            dma((tile_size - 1,)),
            dma((tile_size - 1,)),
            dma((sems,)),
            dma((sems,)),
            dma((sems,)),
            dma((sems,)),
            dma((slots,)),
            dma((slots,)),
        ],
        compiler_params=pltpu.CompilerParams(
            collective_id=1, has_side_effects=True, vmem_limit_bytes=50 * 2**20
        ),
        name="grad_sum",
    )(seam, corner, xg, back, acc, small)


def body(
    inputs,
    grad_out,
    seam_links,
    corner_links,
    dw_weight,
    norm_gain,
    w_in,
    bias_in,
    w_out,
    layer_scale,
):
    samples, local, side, _, channels = inputs.shape
    tiles = samples * local
    x = inputs.reshape(tiles, side * side, channels)
    g = grad_out.reshape(tiles, side * side, channels)
    cell_total = lax.axis_size("tile") * lax.axis_size("rep") * tiles * side * side
    factor = 1.0 / math.sqrt(cell_total)
    strips = gather_halos(x)
    out, xg, back, acc, small = compute(
        seam_links,
        corner_links,
        strips,
        x,
        g,
        dw_weight.T,
        norm_gain[None],
        w_in,
        bias_in[None],
        w_out,
        layer_scale[None],
    )
    xg, gwi, gwo, total = finish(seam_links, corner_links, xg, back, acc, small, factor)
    return (
        out.reshape(inputs.shape),
        xg.reshape(inputs.shape),
        total[0:9].T,
        total[9],
        gwi,
        total[11 : 11 + w_in.shape[1] // channels].reshape(-1),
        gwo,
        total[10],
    )


def solution(mesh):
    placed = (
        P("rep", "tile", None, None, None),
        P("rep", "tile", None, None, None),
        P("tile", None, None),
        P("tile", None, None),
        P(),
        P(),
        P(),
        P(),
        P(),
        P(),
    )
    return jax.shard_map(
        body,
        mesh=mesh,
        in_specs=placed,
        out_specs=(
            P("rep", "tile", None, None, None),
            P("rep", "tile", None, None, None),
            P(),
            P(),
            P(),
            P(),
            P(),
            P(),
        ),
        check_vma=False,
    )
```

time: 217 us -> 91.8 us (0.42)
  Pallas kernels: 0 us -> 74.9 us
  blocking collectives: 68.3 us -> 0 us
  waiting for transfers between devices: 44.4 us -> 0 us
  matrix products: 35.4 us -> 0 us
  other arithmetic: 35.4 us -> 0 us
  between operations: 14.6 us -> 0.68 us
    pallas_call x0 -> x3, Pallas kernels: none -> 74.9 us  [the longest x1 40.8 us: finish(): pl.pallas_call(functools.partial(finish_kernel, side, tiles, factor, orde...]
    psum x1 -> x0, waiting for transfers between devices: 44.4 us -> none  [body(): lax.psum((grad_dw, grad_gain, grad_w_in, grad_bias, grad_w_out, grad_scal...]
    psum x1 -> x0, blocking collectives: 40.8 us -> none  [body(): lax.psum((grad_dw, grad_gain, grad_w_in, grad_bias, grad_w_out, grad_scal...]
    dot_general x6 -> x0, matrix products: 35.4 us -> none  [the longest x1 19.3 us: forward_backward(): jnp.dot(normed, w_in, preferred_element_type=jnp.float32) + bias_in]
    all_gather x4 -> x0, blocking collectives: 27.5 us -> none  [the longest x1 8.66 us: body(): lax.all_gather(back_strips.astype(jnp.bfloat16), 'tile', axis=1, tiled=True)]
    reduce_sum x4 -> x0, other arithmetic: 15.2 us -> none  [the longest x1 8.32 us: forward_backward(): jnp.sum((grad_mixed * window).reshape(-1, channels), axis=0)]
    unnamed x46 -> x25, local copies, waits for them, and re-layouts: 3.7 us -> 14.5 us
    add x2 -> x0, other arithmetic: 7.26 us -> none  [the longest x1 4.49 us: add_to_rims(): target + jnp.where(bottom_mask & left_mask, points[..., 3, :][..., None,...]
  transfers between devices with their start and end apart: 1 -> 0, of which waited for: 1 -> 0; matrix products, arithmetic and copies ran while one was open for 16% -> 0% of each run, Pallas kernels for 0% -> 0%
where the time goes in v1:
time: 91.8 us; the launch traced here: 91.3 us
  Pallas kernels  74.9 us (82%)
  local copies, waits for them, and re-layouts  15.7 us (17%)
    pallas_call x1, Pallas kernels, finish(): pl.pallas_call(functools.partial(finish_kernel, side, tiles, factor, orde...  40.8 us
    pallas_call x1, Pallas kernels, compute(): pl.pallas_call(functools.partial(compute_kernel, side, tiles), out_shape=...  24.8 us
    unnamed x25, local copies, waits for them, and re-layouts  14.5 us
    pallas_call x1, Pallas kernels, gather_halos(): pl.pallas_call(functools.partial(halo_kernel, side, tiles), out_shape=jax...  9.4 us

profile of v1, /device:TPU:1, one launch (start us, length us, event | category | flops | bytes accessed | tf_op | source)
XLA Modules:
  0.0 91.3 jit_solution(6407072996577335430)
XLA Ops:
  0.6 0.8 copy.18.seam_ref
  1.4 0.8 copy.19.corner_ref
  2.2 0.0 copy-start
  2.2 1.2 %copy-done = bf16[1,2,32,32,256]{4,3,2,1,0:T(8,128)(2,1)S(1)} copy-done((bf16[1,2,32,32,256]{4,3,2,1,0:T(8,128)(2,1)S(1)}, bf16[1,2,32,32,256]{4,3,2,1,0:T(8,128)(2,1)}, u32[]{:S(2)}) %copy-start) | copy-done | bytes 1048600
  3.4 0.0 copy-start.1
  3.4 9.4 %halo_gather.1.strips_ref = bf16[8,128,256]{2,1,0:T(8,128)(2,1)S(1)} custom-call(bf16[2,1024,256]{2,1,0:T(8,128)(2,1)S(1)} %bitcast.16), custom_call_target="tpu_custom_call" | custom-call | tf_op jit(solution)/shard_map/halo_gather/pallas_call | solution.py:94
  12.8 0.0 copy-done.1
  12.8 0.0 copy-start.2
  12.8 1.2 %copy-done.2 = bf16[1,2,32,32,256]{4,3,2,1,0:T(8,128)(2,1)S(1)} copy-done((bf16[1,2,32,32,256]{4,3,2,1,0:T(8,128)(2,1)S(1)}, bf16[1,2,32,32,256]{4,3,2,1,0:T(8,128)(2,1)}, u32[]{:S(2)}) %copy-start.2) | copy-done | bytes 1048600
  14.1 0.0 copy-start.3
  14.1 1.0 %copy-done.3 = bf16[256,1024]{1,0:T(8,128)(2,1)S(1)} copy-done((bf16[256,1024]{1,0:T(8,128)(2,1)S(1)}, bf16[256,1024]{1,0:T(8,128)(2,1)}, u32[]{:S(2)}) %copy-start.3) | copy-done | bytes 524312
  15.1 0.0 copy-start.4
  15.1 1.0 %copy-done.4 = bf16[1024,256]{1,0:T(8,128)(2,1)S(1)} copy-done((bf16[1024,256]{1,0:T(8,128)(2,1)S(1)}, bf16[1024,256]{1,0:T(8,128)(2,1)}, u32[]{:S(2)}) %copy-start.4) | copy-done | bytes 524312
  16.1 0.0 copy-start.5
  16.1 0.7 copy-done.5
  16.9 0.0 copy-start.6
  16.9 0.7 copy-done.6
  17.5 0.0 copy-start.7
  17.5 0.7 copy-done.7
  18.2 0.0 copy-start.8
  18.2 0.7 copy-done.8
  18.9 24.8 %block_grads.1 = (bf16[2,1024,256]{2,1,0:T(8,128)(2,1)}, f32[2,1024,256]{2,1,0:T(8,128)}, bf16[2,144,256]{2,1,0:T(8,128)(2,1)S(1)}, f32[16,256,128]{2,1,0:T(8,128)}, f32[16,256]{1,0:T(8,128)S(1)}) custom-call(s32[2,4,3]{2,1,0:T(4,128)S(1)} %copy.18.seam_ref, s32[2,4,2]{2,1,0:T(4,128)S(1)} %copy.19.corner_ref, ...), custom_call_target="tpu_custom_call" | custom-call | tf_op jit(solution)/shard_map/block_grads/pallas_call | solution.py:329
  43.7 40.8 %grad_sum.1 = (f32[2,1024,256]{2,1,0:T(8,128)}, f32[256,1024]{1,0:T(8,128)S(1)}, f32[1024,256]{1,0:T(8,128)S(1)}, f32[16,256]{1,0:T(8,128)S(1)}) custom-call(s32[2,4,3]{2,1,0:T(4,128)S(1)} %copy.18.seam_ref, s32[2,4,2]{2,1,0:T(4,128)S(1)} %copy.19.corner_ref, f32[2,1024,256]{2,1,0:T(8,128)} %get-tuple-element.18.xg_in, ...), custom_call_target="tpu_custom_call" | custom-call | tf_op jit(solution)/shard_map/grad_sum/pallas_call | solution.py:640
  84.4 0.6 fusion
  85.0 0.6 slice_bitcast_fusion
  85.6 0.6 copy.22
  86.2 3.2 %copy.26 = f32[1,2,32,32,256]{4,3,2,1,0:T(8,128)} copy(f32[1,2,32,32,256]{4,3,2,1,0:T(8,128)} %bitcast.23) | data formatting | bytes 4194304
  89.4 1.0 %copy.27 = f32[256,1024]{1,0:T(8,128)} copy(f32[256,1024]{1,0:T(8,128)S(1)} %get-tuple-element.40) | data formatting | bytes 2097152
  90.3 1.0 %copy.28 = f32[1024,256]{1,0:T(8,128)} copy(f32[1024,256]{1,0:T(8,128)S(1)} %get-tuple-element.42) | data formatting | bytes 2097152
  (1 shorter events, 0.0 us)
Async XLA Ops:
  2.2 1.2 %copy-start = (bf16[1,2,32,32,256]{4,3,2,1,0:T(8,128)(2,1)S(1)}, bf16[1,2,32,32,256]{4,3,2,1,0:T(8,128)(2,1)}, u32[]{:S(2)}) copy-start(bf16[1,2,32,32,256]{4,3,2,1,0:T(8,128)(2,1)} %param.10) | copy-start | bytes 3145732
  3.4 9.4 %copy-start.1 = (bf16[1,2,32,32,256]{4,3,2,1,0:T(8,128)(2,1)S(1)}, bf16[1,2,32,32,256]{4,3,2,1,0:T(8,128)(2,1)}, u32[]{:S(2)}) copy-start(bf16[1,2,32,32,256]{4,3,2,1,0:T(8,128)(2,1)} %param.10) | copy-start | bytes 3145732
  12.8 1.2 %copy-start.2 = (bf16[1,2,32,32,256]{4,3,2,1,0:T(8,128)(2,1)S(1)}, bf16[1,2,32,32,256]{4,3,2,1,0:T(8,128)(2,1)}, u32[]{:S(2)}) copy-start(bf16[1,2,32,32,256]{4,3,2,1,0:T(8,128)(2,1)} %param.11) | copy-start | bytes 3145732
  14.1 1.0 %copy-start.3 = (bf16[256,1024]{1,0:T(8,128)(2,1)S(1)}, bf16[256,1024]{1,0:T(8,128)(2,1)}, u32[]{:S(2)}) copy-start(bf16[256,1024]{1,0:T(8,128)(2,1)} %w_in_ref.1) | copy-start | bytes 1572868
  15.1 1.0 %copy-start.4 = (bf16[1024,256]{1,0:T(8,128)(2,1)S(1)}, bf16[1024,256]{1,0:T(8,128)(2,1)}, u32[]{:S(2)}) copy-start(bf16[1024,256]{1,0:T(8,128)(2,1)} %w_out_ref.1) | copy-start | bytes 1572868
  16.1 0.7 copy-start.5
  16.9 0.7 copy-start.6
  17.5 0.7 copy-start.7
  18.2 0.7 copy-start.8

commit v2 on v1

--- a/solution.py
+++ b/solution.py
@@ -34,23 +34,49 @@
     return jnp.where(mask, 1.0, 0.0).astype(BF16)
 
 
-def tile_gather(tiles, buf, send_sem, recv_sem):
+def block_copy(tiles, buf, send_sem, recv_sem, block, to, slot):
+    where = pl.ds(block * tiles, tiles)
+    copy = pltpu.make_async_remote_copy(
+        src_ref=buf.at[where],
+        dst_ref=buf.at[where],
+        send_sem=send_sem.at[slot],
+        recv_sem=recv_sem.at[slot],
+        device_id={"tile": to},
+        device_id_type=MESH,
+    )
+    copy.start()
+    return copy
+
+
+def tile_gather(*refs):
     size = lax.axis_size("tile")
     me = lax.axis_index("tile")
-    mine = pl.ds(me * tiles, tiles)
-    copies = []
-    for k in range(1, size):
-        copy = pltpu.make_async_remote_copy(
-            src_ref=buf.at[mine],
-            dst_ref=buf.at[mine],
-            send_sem=send_sem.at[k - 1],
-            recv_sem=recv_sem.at[k - 1],
-            device_id={"tile": lax.rem(me + k, size)},
-            device_id_type=MESH,
+    far = [
+        block_copy(*refs, me, lax.rem(me + 2 * k, size), k - 1) for k in range(1, size // 2)
+    ]
+    near = block_copy(*refs, me, me + 1 - 2 * lax.rem(me, 2), size // 2 - 1)
+    return far, near
+
+
+def tile_forward(started, *refs):
+    size = lax.axis_size("tile")
+    me = lax.axis_index("tile")
+    far, near = started
+    passed = []
+    for k, copy in enumerate(far, 1):
+        copy.wait_recv()
+        block = lax.rem(me + size - 2 * k, size)
+        passed.append(
+            block_copy(*refs, block, me + 1 - 2 * lax.rem(me, 2), size // 2 - 1 + k)
         )
-        copy.start()
-        copies.append(copy)
-    return copies
+    return far, [near] + passed
+
+
+def tile_end(far, near):
+    for copy in near:
+        copy.wait_recv()
+    for copy in far + near:
+        copy.wait_send()
 
 
 def halo_kernel(side, tiles, x_ref, out_ref, land, send_sem, recv_sem):
@@ -80,9 +106,8 @@
     for t in range(tiles):
         land[me * tiles + t] = dot(sel, x_ref[t]).astype(BF16)
     pl.semaphore_wait(barrier, size - 1)
-    copies = tile_gather(tiles, land, send_sem, recv_sem)
-    for copy in copies:
-        copy.wait()
+    refs = (tiles, land, send_sem, recv_sem)
+    tile_end(*tile_forward(tile_gather(*refs), *refs))
     out_ref[...] = land[...]
 
 
@@ -366,11 +391,10 @@
     orders,
     seam_ref,
     corner_ref,
-    xg_in,
     back_ref,
     acc_ref,
     small_ref,
-    xg_ref,
+    table_ref,
     gwi_ref,
     gwo_ref,
     tot_ref,
@@ -544,7 +568,8 @@
     for part in part_ids:
         flying[part] = start_scatter(part, 0)
         every += flying[part]
-    halo = tile_gather(tiles, land, halo_send, halo_recv)
+    refs = (tiles, land, halo_send, halo_recv)
+    halo = tile_gather(*refs)
     small = start_small(0, small_ref[...])
     every += small
     for s in range(stage_count):
@@ -555,46 +580,35 @@
             else:
                 flying[part] = start_gather(part, s)
             every += flying[part]
+        if s == 0:
+            halo = tile_forward(halo, *refs)
         value = end_small(s, small)
         if s + 1 < stage_count:
             small = start_small(s + 1, value)
             every += small
     tot_ref[...] = value * factor
 
-    for copy in halo:
-        copy.wait()
-    cells = side * side
-    width = SIDES * side + CORNER_ROWS
-    total_rows = land.shape[0] * width
-    home = land[...].reshape(total_rows, land.shape[2])
-    row = iota((width, 1), 0)
-    rr = iota((width, total_rows), 1)
-    cell = iota((cells, 1), 0)
-    i = cell // side
-    j = cell % side
-    r = iota((cells, width), 1)
-    rim = None
-    for s, (on, p) in enumerate(((i == 0, j), (j == last, i), (i == last, j), (j == 0, i))):
-        hit = r == jnp.where(on, s * side + p, -1)
-        rim = hit if rim is None else rim | hit
-    for k, cell_k in enumerate((0, last, cells - 1, cells - side)):
-        rim = rim | (r == jnp.where(cell == cell_k, SIDES * side + k, -1))
-    rim = one_hot(rim)
-    for t in range(tiles):
-        source = jnp.full((width, 1), -1, jnp.int32)
-        for s in range(SIDES):
-            t2, s2, f = seam_ref[t, s, 0], seam_ref[t, s, 1], seam_ref[t, s, 2]
-            flip = f + (1 if s >= 2 else 0) + s2 // 2
-            flip = flip - 2 * (flip // 2)
-            p = row - s * side
-            at = t2 * width + s2 * side + p + flip * (last - 2 * p)
-            source = jnp.where((row >= s * side) & (row < (s + 1) * side), at, source)
-        for k in range(4):
-            t2, k2 = corner_ref[t, k, 0], corner_ref[t, k, 1]
-            at = t2 * width + SIDES * side + k2
-            source = jnp.where(row == SIDES * side + k, at, source)
-        table = dot(one_hot(rr == source), home).astype(BF16)
-        xg_ref[t] = xg_in[t] + dot(rim, table)
+    def return_halos():
+        tile_end(*halo)
+        width = SIDES * side + CORNER_ROWS
+        total_rows = land.shape[0] * width
+        home = land[...].reshape(total_rows, land.shape[2])
+        row = iota((width, 1), 0)
+        rr = iota((width, total_rows), 1)
+        for t in range(tiles):
+            source = jnp.full((width, 1), -1, jnp.int32)
+            for s in range(SIDES):
+                t2, s2, f = seam_ref[t, s, 0], seam_ref[t, s, 1], seam_ref[t, s, 2]
+                flip = f + (1 if s >= 2 else 0) + s2 // 2
+                flip = flip - 2 * (flip // 2)
+                p = row - s * side
+                at = t2 * width + s2 * side + p + flip * (last - 2 * p)
+                source = jnp.where((row >= s * side) & (row < (s + 1) * side), at, source)
+            for k in range(4):
+                t2, k2 = corner_ref[t, k, 0], corner_ref[t, k, 1]
+                at = t2 * width + SIDES * side + k2
+                source = jnp.where(row == SIDES * side + k, at, source)
+            table_ref[t] = dot(one_hot(rr == source), home).astype(BF16)
 
     for s in reversed(range(stage_count)):
         for part in part_ids:
@@ -603,6 +617,8 @@
             if s > 0:
                 flying[part] = start_gather(part, s - 1)
                 every += flying[part]
+        if s == 1:
+            return_halos()
     channels = gwi_ref.shape[0]
     hidden = gwi_ref.shape[1]
     per = channels // 16
@@ -616,17 +632,18 @@
         copy.wait_send()
 
 
-def finish(seam, corner, xg, back, acc, small, factor):
-    tiles, cells, channels = xg.shape
-    side = math.isqrt(cells)
+def finish(seam, corner, side, back, acc, small, factor):
+    tiles, _, channels = back.shape
     tile_size = lax.axis_size("tile")
     rep_size = lax.axis_size("rep")
     acc = acc.reshape(-1, 16, 128)
     hidden = acc.shape[0] * 16 * 128 // (2 * channels)
     core, rest, near, far = digits_of(tile_size, rep_size)
     orders = [(core, rest, near, far), (core, near, rest, far)]
-    if acc.shape[0] < 2 * tile_size * rep_size:
+    if acc.shape[0] < 4 * tile_size * rep_size:
         orders = orders[:1]
+    else:
+        orders = orders * 2
     sems = 0
     rows = 0
     for order in orders:
@@ -640,12 +657,12 @@
     return pl.pallas_call(
         functools.partial(finish_kernel, side, tiles, factor, orders),
         out_shape=(
-            jax.ShapeDtypeStruct(xg.shape, F32),
+            jax.ShapeDtypeStruct(back.shape, BF16),
             jax.ShapeDtypeStruct((channels, hidden), F32),
             jax.ShapeDtypeStruct((hidden, channels), F32),
             jax.ShapeDtypeStruct(small.shape, F32),
         ),
-        in_specs=[SMEM, SMEM] + [VMEM] * 4,
+        in_specs=[SMEM, SMEM] + [VMEM] * 3,
         out_specs=(VMEM,) * 4,
         scratch_shapes=[
             pltpu.VMEM((tile_size * tiles,) + back.shape[1:], BF16),
@@ -667,7 +684,39 @@
             collective_id=1, has_side_effects=True, vmem_limit_bytes=50 * 2**20
         ),
         name="grad_sum",
-    )(seam, corner, xg, back, acc, small)
+    )(seam, corner, back, acc, small)
+
+
+def rim_kernel(side, table_ref, xg_in, xg_ref):
+    last = side - 1
+    cells = side * side
+    width = table_ref.shape[1]
+    cell = iota((cells, 1), 0)
+    i = cell // side
+    j = cell % side
+    r = iota((cells, width), 1)
+    rim = None
+    for s, (on, p) in enumerate(((i == 0, j), (j == last, i), (i == last, j), (j == 0, i))):
+        hit = r == jnp.where(on, s * side + p, -1)
+        rim = hit if rim is None else rim | hit
+    for k, cell_k in enumerate((0, last, cells - 1, cells - side)):
+        rim = rim | (r == jnp.where(cell == cell_k, SIDES * side + k, -1))
+    rim = one_hot(rim)
+    xg_ref[0] = xg_in[0] + dot(rim, table_ref[0])
+
+
+def add_rims(xg, table):
+    tiles, cells, channels = xg.shape
+    block = pl.BlockSpec((1, cells, channels), lambda t: (t, 0, 0))
+    return pl.pallas_call(
+        functools.partial(rim_kernel, math.isqrt(cells)),
+        grid=(tiles,),
+        out_shape=jax.ShapeDtypeStruct(xg.shape, F32),
+        in_specs=[pl.BlockSpec((1,) + table.shape[1:], lambda t: (t, 0, 0)), block],
+        out_specs=block,
+        compiler_params=pltpu.CompilerParams(vmem_limit_bytes=32 * 2**20),
+        name="add_rims",
+    )(table, xg)
 
 
 def body(
@@ -702,7 +751,8 @@
         w_out,
         layer_scale[None],
     )
-    xg, gwi, gwo, total = finish(seam_links, corner_links, xg, back, acc, small, factor)
+    table, gwi, gwo, total = finish(seam_links, corner_links, side, back, acc, small, factor)
+    xg = add_rims(xg, table)
     return (
         out.reshape(inputs.shape),
         xg.reshape(inputs.shape),

time: 91.8 us -> 82.5 us (0.90)
  Pallas kernels: 74.9 us -> 68.8 us
  local copies, waits for them, and re-layouts: 15.7 us -> 12.6 us
    pallas_call x1, Pallas kernels: 40.8 us -> 34.3 us  [finish(): pl.pallas_call(functools.partial(finish_kernel, side, tiles, factor, orde...]
    unnamed x25 -> x26, local copies, waits for them, and re-layouts: 14.5 us -> 11.4 us
    pallas_call x0 -> x1, Pallas kernels: none -> 1.63 us  [add_rims(): pl.pallas_call(functools.partial(rim_kernel, math.isqrt(cells)), grid=(ti...]
    pallas_call x1, Pallas kernels: 9.4 us -> 8.12 us  [gather_halos(): pl.pallas_call(functools.partial(halo_kernel, side, tiles), out_shape=jax...]
where the time goes in v2:
time: 82.5 us; the launch traced here: 82.1 us
  Pallas kernels  68.8 us (83%)
  local copies, waits for them, and re-layouts  12.6 us (15%)
    pallas_call x1, Pallas kernels, finish(): pl.pallas_call(functools.partial(finish_kernel, side, tiles, factor, orde...  34.3 us
    pallas_call x1, Pallas kernels, compute(): pl.pallas_call(functools.partial(compute_kernel, side, tiles), out_shape=...  24.8 us
    unnamed x26, local copies, waits for them, and re-layouts  11.4 us
    pallas_call x1, Pallas kernels, gather_halos(): pl.pallas_call(functools.partial(halo_kernel, side, tiles), out_shape=jax...  8.12 us

profile of v2, /device:TPU:1, one launch (start us, length us, event | category | flops | bytes accessed | tf_op | source)
XLA Modules:
  0.0 82.1 jit_solution(3836655661673027914)
XLA Ops:
  0.6 0.8 copy.18.seam_ref
  1.4 0.8 copy.19.corner_ref
  2.2 0.0 copy-start
  2.2 1.2 %copy-done = bf16[1,2,32,32,256]{4,3,2,1,0:T(8,128)(2,1)S(1)} copy-done((bf16[1,2,32,32,256]{4,3,2,1,0:T(8,128)(2,1)S(1)}, bf16[1,2,32,32,256]{4,3,2,1,0:T(8,128)(2,1)}, u32[]{:S(2)}) %copy-start) | copy-done | bytes 1048600
  3.4 0.0 copy-start.1
  3.4 8.1 %halo_gather.1.strips_ref = bf16[8,128,256]{2,1,0:T(8,128)(2,1)S(1)} custom-call(bf16[2,1024,256]{2,1,0:T(8,128)(2,1)S(1)} %bitcast.16), custom_call_target="tpu_custom_call" | custom-call | tf_op jit(solution)/shard_map/halo_gather/pallas_call | solution.py:119
  11.5 0.0 copy-done.1
  11.5 0.0 copy-start.3
  11.6 1.2 %copy-done.3 = bf16[1,2,32,32,256]{4,3,2,1,0:T(8,128)(2,1)S(1)} copy-done((bf16[1,2,32,32,256]{4,3,2,1,0:T(8,128)(2,1)S(1)}, bf16[1,2,32,32,256]{4,3,2,1,0:T(8,128)(2,1)}, u32[]{:S(2)}) %copy-start.3) | copy-done | bytes 1048600
  12.8 0.0 copy-start.4
  12.8 1.0 %copy-done.4 = bf16[256,1024]{1,0:T(8,128)(2,1)S(1)} copy-done((bf16[256,1024]{1,0:T(8,128)(2,1)S(1)}, bf16[256,1024]{1,0:T(8,128)(2,1)}, u32[]{:S(2)}) %copy-start.4) | copy-done | bytes 524312
  13.8 0.0 copy-start.5
  13.8 1.0 %copy-done.5 = bf16[1024,256]{1,0:T(8,128)(2,1)S(1)} copy-done((bf16[1024,256]{1,0:T(8,128)(2,1)S(1)}, bf16[1024,256]{1,0:T(8,128)(2,1)}, u32[]{:S(2)}) %copy-start.5) | copy-done | bytes 524312
  14.9 0.0 copy-start.6
  14.9 0.7 copy-done.6
  15.6 0.0 copy-start.7
  15.6 0.7 copy-done.7
  16.3 0.0 copy-start.8
  16.3 0.7 copy-done.8
  16.9 0.0 copy-start.9
  16.9 0.7 copy-done.9
  17.6 24.8 %block_grads.1 = (bf16[2,1024,256]{2,1,0:T(8,128)(2,1)}, f32[2,1024,256]{2,1,0:T(8,128)}, bf16[2,144,256]{2,1,0:T(8,128)(2,1)S(1)}, f32[16,256,128]{2,1,0:T(8,128)}, f32[16,256]{1,0:T(8,128)S(1)}) custom-call(s32[2,4,3]{2,1,0:T(4,128)S(1)} %copy.18.seam_ref, s32[2,4,2]{2,1,0:T(4,128)S(1)} %copy.19.corner_ref, ...), custom_call_target="tpu_custom_call" | custom-call | tf_op jit(solution)/shard_map/block_grads/pallas_call | solution.py:354
  42.4 0.0 copy-start.2
  42.4 34.3 %grad_sum.1 = (bf16[2,144,256]{2,1,0:T(8,128)(2,1)S(1)}, f32[256,1024]{1,0:T(8,128)S(1)}, f32[1024,256]{1,0:T(8,128)S(1)}, f32[16,256]{1,0:T(8,128)S(1)}) custom-call(s32[2,4,3]{2,1,0:T(4,128)S(1)} %copy.18.seam_ref, s32[2,4,2]{2,1,0:T(4,128)S(1)} %copy.19.corner_ref, bf16[2,144,256]{2,1,0:T(8,128)(2,1)S(1)} %get-tuple-element.18.back_ref, ...), custom_call_target="tpu_custom_call" | custom-call | tf_op jit(solution)/shard_map/grad_sum/pallas_call | solution.py:657
  76.7 0.0 copy-done.2
  76.7 1.6 %add_rims.1 = f32[2,1024,256]{2,1,0:T(8,128)} custom-call(bf16[2,144,256]{2,1,0:T(8,128)(2,1)S(1)} %get-tuple-element.21.table_ref, f32[2,1024,256]{2,1,0:T(8,128)S(1)} %copy-done.2), custom_call_target="tpu_custom_call" | custom-call | tf_op jit(solution)/shard_map/add_rims/pallas_call | solution.py:711
  78.4 0.6 fusion
  78.9 0.6 slice_bitcast_fusion
  79.5 0.6 copy.22
  80.1 1.0 %copy.25 = f32[256,1024]{1,0:T(8,128)} copy(f32[256,1024]{1,0:T(8,128)S(1)} %get-tuple-element.40) | data formatting | bytes 2097152
  81.1 1.0 %copy.26 = f32[1024,256]{1,0:T(8,128)} copy(f32[1024,256]{1,0:T(8,128)S(1)} %get-tuple-element.42) | data formatting | bytes 2097152
  (1 shorter events, 0.0 us)
Async XLA Ops:
  2.2 1.2 %copy-start = (bf16[1,2,32,32,256]{4,3,2,1,0:T(8,128)(2,1)S(1)}, bf16[1,2,32,32,256]{4,3,2,1,0:T(8,128)(2,1)}, u32[]{:S(2)}) copy-start(bf16[1,2,32,32,256]{4,3,2,1,0:T(8,128)(2,1)} %param.10) | copy-start | bytes 3145732
  3.4 8.1 %copy-start.1 = (bf16[1,2,32,32,256]{4,3,2,1,0:T(8,128)(2,1)S(1)}, bf16[1,2,32,32,256]{4,3,2,1,0:T(8,128)(2,1)}, u32[]{:S(2)}) copy-start(bf16[1,2,32,32,256]{4,3,2,1,0:T(8,128)(2,1)} %param.10) | copy-start | bytes 3145732
  11.5 1.2 %copy-start.3 = (bf16[1,2,32,32,256]{4,3,2,1,0:T(8,128)(2,1)S(1)}, bf16[1,2,32,32,256]{4,3,2,1,0:T(8,128)(2,1)}, u32[]{:S(2)}) copy-start(bf16[1,2,32,32,256]{4,3,2,1,0:T(8,128)(2,1)} %param.11) | copy-start | bytes 3145732
  12.8 1.0 %copy-start.4 = (bf16[256,1024]{1,0:T(8,128)(2,1)S(1)}, bf16[256,1024]{1,0:T(8,128)(2,1)}, u32[]{:S(2)}) copy-start(bf16[256,1024]{1,0:T(8,128)(2,1)} %w_in_ref.1) | copy-start | bytes 1572868
  13.8 1.0 %copy-start.5 = (bf16[1024,256]{1,0:T(8,128)(2,1)S(1)}, bf16[1024,256]{1,0:T(8,128)(2,1)}, u32[]{:S(2)}) copy-start(bf16[1024,256]{1,0:T(8,128)(2,1)} %w_out_ref.1) | copy-start | bytes 1572868
  14.9 0.7 copy-start.6
  15.6 0.7 copy-start.7
  16.3 0.7 copy-start.8
  16.9 0.7 copy-start.9
  42.4 34.3 %copy-start.2 = (f32[2,1024,256]{2,1,0:T(8,128)S(1)}, f32[2,1024,256]{2,1,0:T(8,128)}, u32[]{:S(2)}) copy-start(f32[2,1024,256]{2,1,0:T(8,128)} %get-tuple-element.22.xg_in) | copy-start | bytes 6291460

commit v3 on v2

--- a/solution.py
+++ b/solution.py
@@ -127,7 +127,7 @@
             pltpu.SemaphoreType.DMA((size - 1,)),
         ],
         compiler_params=pltpu.CompilerParams(
-            collective_id=0, has_side_effects=True, vmem_limit_bytes=32 * 2**20
+            collective_id=0, has_side_effects=True, vmem_limit_bytes=60 * 2**20
         ),
         name="halo_gather",
     )(x)
@@ -370,7 +370,7 @@
             pltpu.VMEM((2, 8, channels), F32),
             pltpu.VMEM((8, hidden), F32),
         ],
-        compiler_params=pltpu.CompilerParams(vmem_limit_bytes=50 * 2**20),
+        compiler_params=pltpu.CompilerParams(vmem_limit_bytes=60 * 2**20),
         name="block_grads",
     )(seam, corner, strips, x, g, dw, gain, w_in, bias, w_out, scale)
 
@@ -681,7 +681,7 @@
             dma((slots,)),
         ],
         compiler_params=pltpu.CompilerParams(
-            collective_id=1, has_side_effects=True, vmem_limit_bytes=50 * 2**20
+            collective_id=1, has_side_effects=True, vmem_limit_bytes=60 * 2**20
         ),
         name="grad_sum",
     )(seam, corner, back, acc, small)
@@ -714,7 +714,7 @@
         out_shape=jax.ShapeDtypeStruct(xg.shape, F32),
         in_specs=[pl.BlockSpec((1,) + table.shape[1:], lambda t: (t, 0, 0)), block],
         out_specs=block,
-        compiler_params=pltpu.CompilerParams(vmem_limit_bytes=32 * 2**20),
+        compiler_params=pltpu.CompilerParams(vmem_limit_bytes=60 * 2**20),
         name="add_rims",
     )(table, xg)
 

time: 82.5 us -> 82.1 us (level)
  local copies, waits for them, and re-layouts: 12.6 us -> 6.45 us
  Pallas kernels: 68.8 us -> 74.7 us
    unnamed x26 -> x12, local copies, waits for them, and re-layouts: 11.4 us -> 5.27 us
    pallas_call x1, Pallas kernels: 8.12 us -> 10.1 us  [gather_halos(): pl.pallas_call(functools.partial(halo_kernel, side, tiles), out_shape=jax...]
    pallas_call x1, Pallas kernels: 1.63 us -> 2.96 us  [add_rims(): pl.pallas_call(functools.partial(rim_kernel, math.isqrt(cells)), grid=(ti...]
    pallas_call x1, Pallas kernels: 34.3 us -> 35.6 us  [finish(): pl.pallas_call(functools.partial(finish_kernel, side, tiles, factor, orde...]
    pallas_call x1, Pallas kernels: 24.8 us -> 26 us  [compute(): pl.pallas_call(functools.partial(compute_kernel, side, tiles), out_shape=...]
where the time goes in v3:
time: 82.1 us; the launch traced here: 81.8 us
  Pallas kernels  74.7 us (91%)
  local copies, waits for them, and re-layouts  6.45 us (8%)
    pallas_call x1, Pallas kernels, finish(): pl.pallas_call(functools.partial(finish_kernel, side, tiles, factor, orde...  35.6 us
    pallas_call x1, Pallas kernels, compute(): pl.pallas_call(functools.partial(compute_kernel, side, tiles), out_shape=...  26 us
    pallas_call x1, Pallas kernels, gather_halos(): pl.pallas_call(functools.partial(halo_kernel, side, tiles), out_shape=jax...  10.1 us
    unnamed x12, local copies, waits for them, and re-layouts  5.27 us
    pallas_call x1, Pallas kernels, add_rims(): pl.pallas_call(functools.partial(rim_kernel, math.isqrt(cells)), grid=(ti...  2.96 us

profile of v3, /device:TPU:1, one launch (start us, length us, event | category | flops | bytes accessed | tf_op | source)
XLA Modules:
  0.0 81.8 jit_solution(2960260982635982160)
XLA Ops:
  0.6 1.4 %copy.18.seam_ref = s32[2,4,3]{2,1,0:T(4,128)} copy(s32[2,4,3]{1,0,2:T(2,128)} %param.12) | data formatting | bytes 192 | tf_op args[2]
  2.0 1.4 %copy.19.corner_ref = s32[2,4,2]{2,1,0:T(4,128)} copy(s32[2,4,2]{1,2,0:T(2,128)} %param.13) | data formatting | bytes 128 | tf_op args[3]
  3.4 10.1 %halo_gather.1.strips_ref = bf16[8,128,256]{2,1,0:T(8,128)(2,1)} custom-call(bf16[2,1024,256]{2,1,0:T(8,128)(2,1)} %bitcast.16), custom_call_target="tpu_custom_call" | custom-call | tf_op jit(solution)/shard_map/halo_gather/pallas_call | solution.py:119
  13.5 26.0 %block_grads.1 = (bf16[2,1024,256]{2,1,0:T(8,128)(2,1)}, f32[2,1024,256]{2,1,0:T(8,128)}, bf16[2,144,256]{2,1,0:T(8,128)(2,1)}, f32[16,256,128]{2,1,0:T(8,128)}, f32[16,256]{1,0:T(8,128)}) custom-call(s32[2,4,3]{2,1,0:T(4,128)} %copy.18.seam_ref, s32[2,4,2]{2,1,0:T(4,128)} %copy.19.corner_ref, bf16[8,128,256]{2,1,0:T(8,128)(2,1)} %halo_gather.1.strips_ref, ...), custom_call_target="tpu_custom_call" | custom-call | tf_op jit(solution)/shard_map/block_grads/pallas_call | solution.py:354
  39.5 35.6 %grad_sum.1 = (bf16[2,144,256]{2,1,0:T(8,128)(2,1)}, f32[256,1024]{1,0:T(8,128)}, f32[1024,256]{1,0:T(8,128)}, f32[16,256]{1,0:T(8,128)}) custom-call(s32[2,4,3]{2,1,0:T(4,128)} %copy.18.seam_ref, s32[2,4,2]{2,1,0:T(4,128)} %copy.19.corner_ref, bf16[2,144,256]{2,1,0:T(8,128)(2,1)} %get-tuple-element.18.back_ref, f32[256,16,128]{2,1,0:T(8,128)} %bitcast.19, ...), custom_call_target="tpu_custom_call" | custom-call | tf_op jit(solution)/shard_map/grad_sum/pallas_call | solution.py:657
  75.1 0.0 copy-start.2
  75.1 0.0 copy-start.1
  75.1 3.0 %add_rims.1 = f32[2,1024,256]{2,1,0:T(8,128)} custom-call(bf16[2,144,256]{2,1,0:T(8,128)(2,1)} %get-tuple-element.21.table_ref, f32[2,1024,256]{2,1,0:T(8,128)} %get-tuple-element.22.xg_in), custom_call_target="tpu_custom_call" | custom-call | tf_op jit(solution)/shard_map/add_rims/pallas_call | solution.py:711
  78.1 0.0 copy-start
  78.1 0.0 copy-done.2
  78.1 0.6 fusion
  78.7 0.6 slice_bitcast_fusion
  79.3 0.6 copy.22
  79.9 0.0 copy-done.1
  79.9 1.0 %copy.25 = f32[256,1024]{1,0:T(8,128)} copy(f32[256,1024]{1,0:T(8,128)S(1)} %copy-done.1) | data formatting | bytes 2097152
  80.8 0.0 copy-done
  80.9 1.0 %copy.26 = f32[1024,256]{1,0:T(8,128)} copy(f32[1024,256]{1,0:T(8,128)S(1)} %copy-done) | data formatting | bytes 2097152
  (1 shorter events, 0.0 us)
Async XLA Ops:
  75.1 3.0 %copy-start.2 = (f32[16,256]{1,0:T(8,128)S(1)}, f32[16,256]{1,0:T(8,128)}, u32[]{:S(2)}) copy-start(f32[16,256]{1,0:T(8,128)} %get-tuple-element.23) | copy-start | bytes 49156
  75.1 4.8 %copy-start.1 = (f32[256,1024]{1,0:T(8,128)S(1)}, f32[256,1024]{1,0:T(8,128)}, u32[]{:S(2)}) copy-start(f32[256,1024]{1,0:T(8,128)} %get-tuple-element.40) | copy-start | bytes 3145732
  78.1 2.8 %copy-start = (f32[1024,256]{1,0:T(8,128)S(1)}, f32[1024,256]{1,0:T(8,128)}, u32[]{:S(2)}) copy-start(f32[1024,256]{1,0:T(8,128)} %get-tuple-element.42) | copy-start | bytes 3145732
